TPU v7x, 256 devices: a whole 4x4x8 slice. The times are simulated.
256 devices in a mesh: ra: 16 (over x, z_hi, core), rb: 16 (over y, z_lo).
Axes of the slice: x: 4, y: 4, z: 8 (z_hi: 2, z_lo: 4; z = z_hi * 4 + z_lo), core: 2. Of those that a mesh axis runs over, the one named last changes fastest.
Arguments:
- features_a: bfloat16 [32, 128, 1024], P('ra', 'rb'), may hold values from -600 to 600
- features_b: bfloat16 [32, 128, 1024], P('rb', 'ra'), may hold values from -600 to 600
- weight_one: bfloat16 [16, 81], replicated, may hold values from -16 to 16
- bias_one: float32 [16], replicated, may hold values from -3 to 3
- weight_two: bfloat16 [16, 81], replicated, may hold values from -0.25 to 0.25
- bias_two: float32 [1], replicated, may hold values from -3 to 3
Outputs:
- consensus: float32 [32, 128, 32, 128], P('ra', None, 'rb')
All inputs are finite; a program needn't handle non-finite values.
Results may differ from a plain program's by a relative error of at most 0.0053.
Values may be sent and summed in bfloat16 or wider, within the bound.
A program may use at most 192 MiB of HBM per device.

v0:
```python
import jax
import jax.numpy as jnp
from jax import lax
from jax.sharding import PartitionSpec as P


def extended(cells, sides, width):
    for axis, dim in sides:
        count = lax.axis_size(axis)
        ends = count - 1
        head = lax.slice_in_dim(cells, 0, width, axis=dim)
        tail = lax.slice_in_dim(cells, cells.shape[dim] - width, cells.shape[dim], axis=dim)
        cells = jnp.concatenate(
            [
                lax.ppermute(tail, axis, [(i, (i + 1) % count) for i in range(ends)]),
                cells,
                lax.ppermute(head, axis, [((i + 1) % count, i) for i in range(ends)]),
            ],
            axis=dim,
        )
    return cells


def normalize(features):
    values = features.astype(jnp.float32)
    scale = lax.rsqrt(jnp.sum(values * values, axis=-1, keepdims=True) + 1e-06)
    return (values * scale).astype(jnp.bfloat16)


def correlate(norm_a, norm_b):
    gathered = lax.all_gather(norm_a, "rb", axis=1, tiled=True)
    channels = gathered.shape[2]
    flat_a = gathered.reshape(-1, channels)
    piece = lax.all_gather(norm_b, "ra", axis=1, tiled=True)
    product = lax.dot_general(
        flat_a,
        piece.reshape(-1, channels),
        (((1,), (1,)), ((), ())),
        preferred_element_type=jnp.float32,
    )
    return product.reshape(
        gathered.shape[0], gathered.shape[1], piece.shape[0], piece.shape[1]
    ).astype(jnp.bfloat16)


def pad_columns(volume):
    return jnp.pad(volume, ((0, 0), (1, 1), (0, 0), (1, 1)))


def first_layer(volume, weight_one, bias_one, out_rows, out_k):
    width_j = volume.shape[1] - 2
    width_l = volume.shape[3] - 2

    def first_one_row(row_start):
        block = lax.dynamic_slice_in_dim(volume, row_start, 3, 0)
        patches = jnp.stack(
            [
                block[t_i, t_j : t_j + width_j, t_k : t_k + out_k, t_l : t_l + width_l]
                for t_i in range(3)
                for t_j in range(3)
                for t_k in range(3)
                for t_l in range(3)
            ]
        )
        before = lax.dot_general(
            weight_one, patches, (((1,), (0,)), ((), ())), preferred_element_type=jnp.float32
        )
        return jax.nn.relu(before + bias_one[:, None, None, None])

    return lax.map(first_one_row, jnp.arange(out_rows, dtype=jnp.int32))


def second_sums(hidden_pad, weight_two, out_rows, out_k):
    width_j = hidden_pad.shape[2] - 2
    width_l = hidden_pad.shape[4] - 2

    def second_one_row(row_start):
        total = jnp.zeros((width_j, out_k, width_l), jnp.float32)
        for t_i in range(3):
            plane = lax.dynamic_index_in_dim(hidden_pad, row_start + t_i, 0, keepdims=False)
            taps = lax.dot_general(
                weight_two[:, 27 * t_i : 27 * t_i + 27],
                plane,
                (((0,), (0,)), ((), ())),
                preferred_element_type=jnp.float32,
            )
            for t_j in range(3):
                for t_k in range(3):
                    for t_l in range(3):
                        total = (
                            total
                            + taps[
                                9 * t_j + 3 * t_k + t_l,
                                t_j : t_j + width_j,
                                t_k : t_k + out_k,
                                t_l : t_l + width_l,
                            ]
                        )
        return total

    return lax.map(second_one_row, jnp.arange(out_rows, dtype=jnp.int32))


def second_layer(hidden_pad, weight_two, bias_two, out_rows, out_k):
    return jax.nn.relu(second_sums(hidden_pad, weight_two, out_rows, out_k) + bias_two[0])


def per_device(features_a, features_b, weight_one, bias_one, weight_two, bias_two):
    norm_a = normalize(features_a)
    norm_b = normalize(features_b)
    rows_a = norm_a.shape[0]
    rows_b = norm_b.shape[0]
    volume = correlate(norm_a, norm_b)
    padded = extended(volume, (("ra", 0), ("rb", 2)), 1)
    hidden = first_layer(pad_columns(padded), weight_one, bias_one, rows_a, rows_b).astype(
        jnp.bfloat16
    )
    hidden = extended(hidden, (("ra", 0), ("rb", 3)), 1)
    hidden = jnp.pad(hidden, ((0, 0), (0, 0), (1, 1), (0, 0), (1, 1)))
    return second_layer(hidden, weight_two, bias_two, rows_a, rows_b)


def solution(mesh):
    return jax.shard_map(
        per_device,
        mesh=mesh,
        in_specs=(P("ra", "rb", None), P("rb", "ra", None), P(), P(), P(), P()),
        out_specs=P("ra", None, "rb", None),
        check_vma=False,
    )
```

profile of v0, /device:TPU:232, one launch (start us, length us, event | category | flops | bytes accessed | tf_op | source)
XLA Modules:
  0.0 701.4 jit_solution(13057398529258511894)
XLA Ops:
  1.7 36.8 %all_gather.6 = bf16[2,128,1024]{2,1,0:T(8,128)(2,1)S(1)} all-gather(bf16[2,8,1024]{2,1,0:T(8,128)(2,1)S(1)} %fusion.41), channel_id=1, replica_groups=mesh['ra'=16,'rb'=16] {'rb'}, dimensions={1}, use_global_device_ids=true | all-gather | bytes 557056 | tf_op jit(solution)/shard_map/all_gather | solution.py:31
  40.2 27.3 %all_gather.7 = bf16[2,128,1024]{2,1,0:T(8,128)(2,1)S(1)} all-gather(bf16[2,8,1024]{2,1,0:T(8,128)(2,1)S(1)} %fusion.43), channel_id=1, replica_groups=mesh['ra'=16,'rb'=16] {'ra'}, dimensions={1}, use_global_device_ids=true | all-gather | bytes 557056 | tf_op jit(solution)/shard_map/all_gather | solution.py:34
  70.2 9.7 %collective-permute-start.1 = (bf16[1,128,2,128]{3,1,2,0:T(8,128)(2,1)S(1)}, bf16[1,128,2,128]{3,1,2,0:T(8,128)(2,1)S(1)}, u32[]{:S(2)}, u32[]{:S(2)}) collective-permute-start(bf16[1,128,2,128]{3,1,2,0:T(8,128)(2,1)S(1)} %get-tuple-element.226), channel_id=1, source_target_pairs={{16,0},{32,16},{48,32},{64,48},{80,64},{96,80},{112,96},{128,112},... | collective-permute-start | bytes 196616 | tf_op jit(solution)/shard_map/ppermute | solution.py:17
  81.8 5.7 collective-permute-start.2
  90.6 7.8 %collective-permute-done.3 = bf16[4,128,1,128]{3,1,2,0:T(8,128)(2,1)} collective-permute-done((bf16[4,128,1,128]{3,1,2,0:T(8,128)(2,1)S(1)}, bf16[4,128,1,128]{3,1,2,0:T(8,128)(2,1)}, u32[]{:S(2)}, u32[]{:S(2)}) %collective-permute-start.3) | collective-permute-done | bytes 131104 | tf_op jit(solution)/shard_map/ppermute | solution.py:17
  100.3 225.3 %while.24 = (s32[]{:T(128)}, bf16[2,16,128,2,128]{4,1,3,2,0:T(8,128)(2,1)S(1)}, s32[2]{0:T(128)S(1)}, bf16[4,130,4,130]{3,1,2,0:T(8,128)(2,1)S(1)}, bf16[16,81]{1,0:T(8,128)(2,1)S(1)}, /*index=5*/f32[16]{0:T(128)S(1)}) while((s32[]{:T(128)}, bf16[2,16,128,2,128]{4,1,3,2,0:T(8,128)(2,1)S(1)}, s32[2]{0:T(128)S(1)}, ...), condition=%wide.region_3.4_spmd.clone, body=%wide.region_2.3_spmd.sunk.clone | while | flops 85983240 | bytes 39260856 | solution.py:70
  167.6 41.6 %stack.5 = bf16[81,128,2,128]{3,0,2,1:T(8,128)(2,1)} concatenate(bf16[1,128,2,128]{3,0,2,1:T(2,128)(2,1)S(1)} %copy.263, bf16[1,128,2,128]{3,0,2,1:T(2,128)(2,1)S(1)} %copy.264, bf16[1,128,2,128]{3,0,2,1:T(2,128)(2,1)} %copy.265, bf16[1,128,2,128]{3,0,2,1:T(2,128)(2,1)} %copy.266, bf16[1,128,2,128]{3,0,2,1:T(2,128)(2,1)} %copy.267, bf16[1,128,2,128]{3,0,2,1:T(2,128)(2,1)} %copy.268, ...), dimensions={0} | concatenate | bytes 10616832 | tf_op jit(solution)/shard_map/while/body/eval_jaxpr/stack | solution.py:56
  280.2 41.6 %stack.5 = bf16[81,128,2,128]{3,0,2,1:T(8,128)(2,1)} concatenate(bf16[1,128,2,128]{3,0,2,1:T(2,128)(2,1)S(1)} %copy.263, bf16[1,128,2,128]{3,0,2,1:T(2,128)(2,1)S(1)} %copy.264, bf16[1,128,2,128]{3,0,2,1:T(2,128)(2,1)} %copy.265, bf16[1,128,2,128]{3,0,2,1:T(2,128)(2,1)} %copy.266, bf16[1,128,2,128]{3,0,2,1:T(2,128)(2,1)} %copy.267, bf16[1,128,2,128]{3,0,2,1:T(2,128)(2,1)} %copy.268, ...), dimensions={0} | concatenate | bytes 10616832 | tf_op jit(solution)/shard_map/while/body/eval_jaxpr/stack | solution.py:56
  329.8 5.7 collective-permute-start.5
  335.5 28.8 %collective-permute-done.4 = bf16[1,16,128,2,128]{4,1,3,2,0:T(8,128)(2,1)S(1)} collective-permute-done((bf16[1,16,128,2,128]{4,1,3,2,0:T(8,128)(2,1)S(1)}, bf16[1,16,128,2,128]{4,1,3,2,0:T(8,128)(2,1)S(1)}, u32[]{:S(2)}, u32[]{:S(2)}) %collective-permute-start.4) | collective-permute-done | bytes 1048608 | tf_op jit(solution)/shard_map/ppermute | solution.py:15
  368.5 4.9 collective-permute-start.6
  373.5 9.9 %collective-permute-start.7 = (bf16[4,16,128,1,128]{4,1,3,2,0:T(8,128)(2,1)}, bf16[4,16,128,1,128]{4,1,3,2,0:T(8,128)(2,1)}, u32[]{:S(2)}, u32[]{:S(2)}) collective-permute-start(bf16[4,16,128,1,128]{4,1,3,2,0:T(8,128)(2,1)} %get-tuple-element.220), channel_id=1, source_target_pairs={{1,0},{2,1},{3,2},{4,3},{5,4},{6,5},{7,6},{8,7},{9,8},{10,9},{11,1... | collective-permute-start | bytes 6291464 | tf_op jit(solution)/shard_map/ppermute | solution.py:17
  384.0 39.5 %collective-permute-done.6 = bf16[4,16,128,1,128]{4,1,3,2,0:T(8,128)(2,1)} collective-permute-done((bf16[4,16,128,1,128]{4,1,3,2,0:T(8,128)(2,1)}, bf16[4,16,128,1,128]{4,1,3,2,0:T(8,128)(2,1)}, u32[]{:S(2)}, u32[]{:S(2)}) %collective-permute-start.6) | collective-permute-done | bytes 2097184 | tf_op jit(solution)/shard_map/ppermute | solution.py:15
  423.5 86.5 %collective-permute-done.7 = bf16[4,16,128,1,128]{4,1,3,2,0:T(8,128)(2,1)} collective-permute-done((bf16[4,16,128,1,128]{4,1,3,2,0:T(8,128)(2,1)}, bf16[4,16,128,1,128]{4,1,3,2,0:T(8,128)(2,1)}, u32[]{:S(2)}, u32[]{:S(2)}) %collective-permute-start.7) | collective-permute-done | bytes 2097184 | tf_op jit(solution)/shard_map/ppermute | solution.py:17
  510.0 22.6 %select_maximum_fusion = bf16[4,16,130,4,130]{4,1,3,2,0:T(8,128)(2,1)} fusion(bf16[4,16,128,1,128]{4,1,3,2,0:T(8,128)(2,1)} %collective-permute-done.7, bf16[4,16,128,1,128]{4,1,3,2,0:T(8,128)(2,1)} %collective-permute-done.6, bf16[1,16,128,2,128]{4,1,3,2,0:T(8,128)(2,1)} %copy-done, bf16[2,16,128,2,128]{4,1,3,2,0:T(8,128)(2,1)S(1)} %get-tuple-element.103, ...), kind=kLoop, calls=%fused_computation.165 | loop fusion | flops 116812800 | bytes 17041408 | tf_op jit(solution)/shard_map/concatenate | solution.py:13
  532.6 168.0 %while.25 = (s32[]{:T(128)}, f32[2,128,2,128]{3,2,1,0:T(2,128)S(1)}, s32[2]{0:T(128)S(1)}, bf16[4,16,130,4,130]{4,1,3,2,0:T(8,128)(2,1)}, bf16[16,81]{1,0:T(8,128)(2,1)S(1)}) while((s32[]{:T(128)}, f32[2,128,2,128]{3,2,1,0:T(2,128)S(1)}, s32[2]{0:T(128)S(1)}, bf16[4,16,130,4,130]{4,1,3,2,0:T(8,128)(2,1)}, ...), condition=%wide.region_5.6_spmd.clone, body=%wide.region_4.5_spmd.sunk.clone | while | flops 177840640 | bytes 45699956 | solution.py:101
  534.5 10.6 %convolution_bitcast_fusion.10 = f32[27,130,4,130]{3,0,2,1:T(8,128)} fusion(bf16[4,16,130,4,130]{4,1,3,2,0:T(8,128)(2,1)} %get-tuple-element.604, s32[]{:T(128)S(6)} %select_n.32, bf16[16,81]{1,0:T(8,128)(2,1)S(1)} %get-tuple-element.605), kind=kOutput, calls=%fused_computation.60.clone.1.clone | convolution fusion | flops 58406400 | bytes 11563236 | tf_op jit(solution)/shard_map/while/body/eval_jaxpr/dot_general | solution.py:81
  546.4 10.5 %convolution_bitcast_fusion.9 = f32[27,130,4,130]{3,0,2,1:T(8,128)} fusion(bf16[4,16,130,4,130]{4,1,3,2,0:T(8,128)(2,1)} %get-tuple-element.604, s32[]{:T(128)S(6)} %select_n.31, bf16[16,81]{1,0:T(8,128)(2,1)S(1)} %get-tuple-element.605), kind=kOutput, calls=%fused_computation.59.clone.1.clone | convolution fusion | flops 58406400 | bytes 11563236 | tf_op jit(solution)/shard_map/while/body/eval_jaxpr/dot_general | solution.py:81
  558.8 10.4 %convolution_bitcast_fusion.11 = f32[27,130,4,130]{3,0,2,1:T(8,128)} fusion(bf16[4,16,130,4,130]{4,1,3,2,0:T(8,128)(2,1)} %get-tuple-element.604, s32[]{:T(128)S(6)} %select_n.33, bf16[16,81]{1,0:T(8,128)(2,1)S(1)} %get-tuple-element.605), kind=kOutput, calls=%fused_computation.61.clone.1.clone | convolution fusion | flops 58406400 | bytes 11563236 | tf_op jit(solution)/shard_map/while/body/eval_jaxpr/dot_general | solution.py:81
  569.2 47.3 %slice_add_fusion.82 = f32[1,128,2,128]{3,0,2,1:T(1,128)S(1)} fusion(f32[27,130,4,130]{3,0,2,1:T(8,128)} %convolution_bitcast_fusion.9, f32[27,130,4,130]{3,0,2,1:T(8,128)} %convolution_bitcast_fusion.10, f32[27,130,4,130]{3,0,2,1:T(8,128)} %convolution_bitcast_fusion.11), kind=kLoop, calls=%fused_computation.68.clone.1.clone | loop fusion | flops 2621440 | bytes 10747904 | tf_op jit(solution)/shard_map/while/body/eval_jaxpr/add | solution.py:91
  618.5 10.6 %convolution_bitcast_fusion.10 = f32[27,130,4,130]{3,0,2,1:T(8,128)} fusion(bf16[4,16,130,4,130]{4,1,3,2,0:T(8,128)(2,1)} %get-tuple-element.604, s32[]{:T(128)S(6)} %select_n.32, bf16[16,81]{1,0:T(8,128)(2,1)S(1)} %get-tuple-element.605), kind=kOutput, calls=%fused_computation.60.clone.1.clone | convolution fusion | flops 58406400 | bytes 11563236 | tf_op jit(solution)/shard_map/while/body/eval_jaxpr/dot_general | solution.py:81
  630.4 10.5 %convolution_bitcast_fusion.9 = f32[27,130,4,130]{3,0,2,1:T(8,128)} fusion(bf16[4,16,130,4,130]{4,1,3,2,0:T(8,128)(2,1)} %get-tuple-element.604, s32[]{:T(128)S(6)} %select_n.31, bf16[16,81]{1,0:T(8,128)(2,1)S(1)} %get-tuple-element.605), kind=kOutput, calls=%fused_computation.59.clone.1.clone | convolution fusion | flops 58406400 | bytes 11563236 | tf_op jit(solution)/shard_map/while/body/eval_jaxpr/dot_general | solution.py:81
  642.8 10.4 %convolution_bitcast_fusion.11 = f32[27,130,4,130]{3,0,2,1:T(8,128)} fusion(bf16[4,16,130,4,130]{4,1,3,2,0:T(8,128)(2,1)} %get-tuple-element.604, s32[]{:T(128)S(6)} %select_n.33, bf16[16,81]{1,0:T(8,128)(2,1)S(1)} %get-tuple-element.605), kind=kOutput, calls=%fused_computation.61.clone.1.clone | convolution fusion | flops 58406400 | bytes 11563236 | tf_op jit(solution)/shard_map/while/body/eval_jaxpr/dot_general | solution.py:81
  653.2 47.3 %slice_add_fusion.82 = f32[1,128,2,128]{3,0,2,1:T(1,128)S(1)} fusion(f32[27,130,4,130]{3,0,2,1:T(8,128)} %convolution_bitcast_fusion.9, f32[27,130,4,130]{3,0,2,1:T(8,128)} %convolution_bitcast_fusion.10, f32[27,130,4,130]{3,0,2,1:T(8,128)} %convolution_bitcast_fusion.11), kind=kLoop, calls=%fused_computation.68.clone.1.clone | loop fusion | flops 2621440 | bytes 10747904 | tf_op jit(solution)/shard_map/while/body/eval_jaxpr/add | solution.py:91
  (208 shorter events, 161.2 us)
Async XLA Ops:
  0.0 100.3 %copy-start.3 = (bf16[16,81]{1,0:T(8,128)(2,1)S(1)}, bf16[16,81]{1,0:T(8,128)(2,1)}, u32[]{:S(2)}) copy-start(bf16[16,81]{1,0:T(8,128)(2,1)} %param.12) | copy-start | bytes 7780
  0.0 100.3 %copy-start.4 = (f32[16]{0:T(128)S(1)}, f32[16]{0:T(128)}, u32[]{:S(2)}) copy-start(f32[16]{0:T(128)} %param.13) | copy-start | bytes 196
  67.9 12.0 %collective-permute-start = (bf16[1,128,2,128]{3,1,2,0:T(8,128)(2,1)S(1)}, bf16[1,128,2,128]{3,1,2,0:T(8,128)(2,1)S(1)}, u32[]{:S(2)}, u32[]{:S(2)}) collective-permute-start(bf16[1,128,2,128]{3,1,2,0:T(8,128)(2,1)S(1)} %get-tuple-element.225), channel_id=1, source_target_pairs={{0,16},{16,32},{32,48},{48,64},{64,80},{80,96},{96,112},{112,128},... | collective-permute-start | bytes 196616 | tf_op jit(solution)/shard_map/ppermute | solution.py:15
  70.2 11.6 %collective-permute-start.1 = (bf16[1,128,2,128]{3,1,2,0:T(8,128)(2,1)S(1)}, bf16[1,128,2,128]{3,1,2,0:T(8,128)(2,1)S(1)}, u32[]{:S(2)}, u32[]{:S(2)}) collective-permute-start(bf16[1,128,2,128]{3,1,2,0:T(8,128)(2,1)S(1)} %get-tuple-element.226), channel_id=1, source_target_pairs={{16,0},{32,16},{48,32},{64,48},{80,64},{96,80},{112,96},{128,112},... | collective-permute-start | bytes 196616 | tf_op jit(solution)/shard_map/ppermute | solution.py:17
  81.8 8.2 %collective-permute-start.2 = (bf16[4,128,1,128]{3,1,2,0:T(8,128)(2,1)S(1)}, bf16[4,128,1,128]{3,1,2,0:T(8,128)(2,1)S(1)}, u32[]{:S(2)}, u32[]{:S(2)}) collective-permute-start(bf16[4,128,1,128]{3,1,2,0:T(8,128)(2,1)S(1)} %get-tuple-element.223), channel_id=1, source_target_pairs={{0,1},{1,2},{2,3},{3,4},{4,5},{5,6},{6,7},{7,8},{8,9},{9,10},{10,1... | collective-permute-start | bytes 393224 | tf_op jit(solution)/shard_map/ppermute | solution.py:15
  87.5 11.0 %collective-permute-start.3 = (bf16[4,128,1,128]{3,1,2,0:T(8,128)(2,1)S(1)}, bf16[4,128,1,128]{3,1,2,0:T(8,128)(2,1)}, u32[]{:S(2)}, u32[]{:S(2)}) collective-permute-start(bf16[4,128,1,128]{3,1,2,0:T(8,128)(2,1)S(1)} %get-tuple-element.224), channel_id=1, source_target_pairs={{1,0},{2,1},{3,2},{4,3},{5,4},{6,5},{7,6},{8,7},{9,8},{10,9},{11,1... | collective-permute-start | bytes 393224 | tf_op jit(solution)/shard_map/ppermute | solution.py:17
  90.0 0.7 copy-start.2
  326.0 38.3 %collective-permute-start.4 = (bf16[1,16,128,2,128]{4,1,3,2,0:T(8,128)(2,1)S(1)}, bf16[1,16,128,2,128]{4,1,3,2,0:T(8,128)(2,1)S(1)}, u32[]{:S(2)}, u32[]{:S(2)}) collective-permute-start(bf16[1,16,128,2,128]{4,1,3,2,0:T(8,128)(2,1)S(1)} %get-tuple-element.221), channel_id=1, source_target_pairs={{0,16},{16,32},{32,48},{48,64},{64,80},{80,96},{96,112},{112,128},... | collective-permute-start | bytes 3145736 | tf_op jit(solution)/shard_map/ppermute | solution.py:15
  329.8 34.5 %collective-permute-start.5 = (bf16[1,16,128,2,128]{4,1,3,2,0:T(8,128)(2,1)S(1)}, bf16[1,16,128,2,128]{4,1,3,2,0:T(8,128)(2,1)S(1)}, u32[]{:S(2)}, u32[]{:S(2)}) collective-permute-start(bf16[1,16,128,2,128]{4,1,3,2,0:T(8,128)(2,1)S(1)} %get-tuple-element.222), channel_id=1, source_target_pairs={{16,0},{32,16},{48,32},{64,48},{80,64},{96,80},{112,96},{128,112},... | collective-permute-start | bytes 3145736 | tf_op jit(solution)/shard_map/ppermute | solution.py:17
  364.3 1.0 copy-start
  368.5 55.0 %collective-permute-start.6 = (bf16[4,16,128,1,128]{4,1,3,2,0:T(8,128)(2,1)}, bf16[4,16,128,1,128]{4,1,3,2,0:T(8,128)(2,1)}, u32[]{:S(2)}, u32[]{:S(2)}) collective-permute-start(bf16[4,16,128,1,128]{4,1,3,2,0:T(8,128)(2,1)} %get-tuple-element.219), channel_id=1, source_target_pairs={{0,1},{1,2},{2,3},{3,4},{4,5},{5,6},{6,7},{7,8},{8,9},{9,10},{10,1... | collective-permute-start | bytes 6291464 | tf_op jit(solution)/shard_map/ppermute | solution.py:15
  373.5 136.6 %collective-permute-start.7 = (bf16[4,16,128,1,128]{4,1,3,2,0:T(8,128)(2,1)}, bf16[4,16,128,1,128]{4,1,3,2,0:T(8,128)(2,1)}, u32[]{:S(2)}, u32[]{:S(2)}) collective-permute-start(bf16[4,16,128,1,128]{4,1,3,2,0:T(8,128)(2,1)} %get-tuple-element.220), channel_id=1, source_target_pairs={{1,0},{2,1},{3,2},{4,3},{5,4},{6,5},{7,6},{8,7},{9,8},{10,9},{11,1... | collective-permute-start | bytes 6291464 | tf_op jit(solution)/shard_map/ppermute | solution.py:17
  384.0 148.6 %copy-start.1 = (bf16[16,81]{1,0:T(8,128)(2,1)S(1)}, bf16[16,81]{1,0:T(8,128)(2,1)}, u32[]{:S(2)}) copy-start(bf16[16,81]{1,0:T(8,128)(2,1)} %param.14) | copy-start | bytes 7780
where the time goes:
time: 708 us; the launch traced here: 701 us
  local copies, waits for them, and re-layouts  220 us (31%)
  waiting for transfers between devices  165 us (23%)
  other arithmetic  124 us (18%)
  matrix products  70.7 us (10%)
  blocking collectives  64.1 us (9%)
  starting transfers between devices  43.8 us (6%)
  loops' own time  13.4 us (2%)
    while x162, local copies, waits for them, and re-layouts  120 us
    ppermute x4, waiting for transfers between devices, extended(): lax.ppermute(head, axis, [((i + 1) % count, i) for i in range(ends)])  96.3 us
    add x2, other arithmetic, second_one_row(): total + taps[9 * t_j + 3 * t_k + t_l, t_j:t_j + width_j, t_k:t_k + out_k,...  94.6 us
    another operation x2, local copies, waits for them, and re-layouts, first_one_row(): jnp.stack([block[t_i, t_j:t_j + width_j, t_k:t_k + out_k, t_l:t_l + width...  83.1 us
    ppermute x4, waiting for transfers between devices, extended(): lax.ppermute(tail, axis, [(i, (i + 1) % count) for i in range(ends)])  68.9 us
    dot_general x6, matrix products, second_one_row(): lax.dot_general(weight_two[:, 27 * t_i:27 * t_i + 27], plane, (((0,), (0,...  63 us
    all_gather x1, blocking collectives, correlate(): gathered = lax.all_gather(norm_a, 'rb', axis=1, tiled=True)  36.8 us
    all_gather x1, blocking collectives, correlate(): piece = lax.all_gather(norm_b, 'ra', axis=1, tiled=True)  27.3 us
  transfers between devices with their start and end apart: 8, of which 6 were waited for; matrix products, arithmetic and copies ran while one was open for 0% of the time, Pallas kernels for 0%

commit v1 on v0

--- a/solution.py
+++ b/solution.py
@@ -28,7 +28,9 @@
 
 
 def correlate(norm_a, norm_b):
-    gathered = lax.all_gather(norm_a, "rb", axis=1, tiled=True)
+    gathered = jnp.concatenate(
+        lax.all_to_all(jnp.stack([norm_a] * lax.axis_size("rb")), "rb", 0, 0), axis=1
+    )
     channels = gathered.shape[2]
     flat_a = gathered.reshape(-1, channels)
     piece = lax.all_gather(norm_b, "ra", axis=1, tiled=True)

time: 708 us -> 651 us (0.919)
  the two profiles are of different devices: /device:TPU:232 before, /device:TPU:39 now
where the time goes in v1:
time: 651 us; the launch traced here: 644 us
  local copies, waits for them, and re-layouts  221 us (34%)
  waiting for transfers between devices  146 us (22%)
  other arithmetic  126 us (19%)
  matrix products  70.7 us (11%)
  starting transfers between devices  35 us (5%)
  blocking collectives  31.7 us (5%)
  loops' own time  13.4 us (2%)
    while x162, local copies, waits for them, and re-layouts  120 us
    add x2, other arithmetic, second_one_row(): total + taps[9 * t_j + 3 * t_k + t_l, t_j:t_j + width_j, t_k:t_k + out_k,...  96.7 us
    another operation x2, local copies, waits for them, and re-layouts, first_one_row(): jnp.stack([block[t_i, t_j:t_j + width_j, t_k:t_k + out_k, t_l:t_l + width...  83.1 us
    ppermute x4, waiting for transfers between devices, extended(): lax.ppermute(tail, axis, [(i, (i + 1) % count) for i in range(ends)])  80.2 us
    ppermute x4, waiting for transfers between devices, extended(): lax.ppermute(head, axis, [((i + 1) % count, i) for i in range(ends)])  66.1 us
    dot_general x6, matrix products, second_one_row(): lax.dot_general(weight_two[:, 27 * t_i:27 * t_i + 27], plane, (((0,), (0,...  63 us
    all_gather x1, blocking collectives, correlate(): piece = lax.all_gather(norm_b, 'ra', axis=1, tiled=True)  31.7 us
    concatenate x4, other arithmetic, extended(): jnp.concatenate([lax.ppermute(tail, axis, [(i, (i + 1) % count) for i in...  24.9 us
  transfers between devices with their start and end apart: 9, of which 5 were waited for; matrix products, arithmetic and copies ran while one was open for 0% of the time, Pallas kernels for 0%

profile of v1, /device:TPU:39, one launch (start us, length us, event | category | flops | bytes accessed | tf_op | source)
XLA Modules:
  0.0 644.4 jit_solution(11417510354004948233)
XLA Ops:
  2.6 8.1 %all-to-all-start = ((bf16[16,2,8,1024]{3,2,1,0:T(8,128)(2,1)}), bf16[16,2,8,1024]{3,2,1,0:T(8,128)(2,1)S(1)}, u32[]{:S(2)}, u32[]{:S(2)}) async-start(bf16[16,2,8,1024]{3,2,1,0:T(8,128)(2,1)} %stack.4), calls=%async_computation | async-start | bytes 1048576 | tf_op jit(solution)/shard_map/all_to_all | solution.py:32
  12.4 31.7 %all_gather.3 = bf16[2,128,1024]{2,1,0:T(8,128)(2,1)S(1)} all-gather(bf16[2,8,1024]{2,1,0:T(8,128)(2,1)S(1)} %fusion.44), channel_id=1, replica_groups=mesh['ra'=16,'rb'=16] {'ra'}, dimensions={1}, use_global_device_ids=true | all-gather | bytes 557056 | tf_op jit(solution)/shard_map/all_gather | solution.py:36
  49.7 7.6 %collective-permute-done.1 = bf16[1,128,2,128]{3,1,2,0:T(8,128)(2,1)S(1)} collective-permute-done((bf16[1,128,2,128]{3,1,2,0:T(8,128)(2,1)S(1)}, bf16[1,128,2,128]{3,1,2,0:T(8,128)(2,1)S(1)}, u32[]{:S(2)}, u32[]{:S(2)}) %collective-permute-start.1) | collective-permute-done | bytes 65568 | tf_op jit(solution)/shard_map/ppermute | solution.py:17
  57.3 6.2 collective-permute-start.2
  66.2 4.9 collective-permute-done.3
  72.9 225.3 %while.24 = (s32[]{:T(128)}, bf16[2,16,128,2,128]{4,1,3,2,0:T(8,128)(2,1)S(1)}, s32[2]{0:T(128)S(1)}, bf16[4,130,4,130]{3,1,2,0:T(8,128)(2,1)S(1)}, bf16[16,81]{1,0:T(8,128)(2,1)S(1)}, /*index=5*/f32[16]{0:T(128)S(1)}) while((s32[]{:T(128)}, bf16[2,16,128,2,128]{4,1,3,2,0:T(8,128)(2,1)S(1)}, s32[2]{0:T(128)S(1)}, ...), condition=%wide.region_3.4_spmd.clone, body=%wide.region_2.3_spmd.sunk.clone | while | flops 85983240 | bytes 39260856 | solution.py:72
  75.5 4.8 fusion.72
  140.2 41.6 %stack.7 = bf16[81,128,2,128]{3,0,2,1:T(8,128)(2,1)} concatenate(bf16[1,128,2,128]{3,0,2,1:T(2,128)(2,1)S(1)} %copy.271, bf16[1,128,2,128]{3,0,2,1:T(2,128)(2,1)S(1)} %copy.272, bf16[1,128,2,128]{3,0,2,1:T(2,128)(2,1)} %copy.273, bf16[1,128,2,128]{3,0,2,1:T(2,128)(2,1)} %copy.274, bf16[1,128,2,128]{3,0,2,1:T(2,128)(2,1)} %copy.275, bf16[1,128,2,128]{3,0,2,1:T(2,128)(2,1)} %copy.276, ...), dimensions={0} | concatenate | bytes 10616832 | tf_op jit(solution)/shard_map/while/body/eval_jaxpr/stack | solution.py:58
  188.0 4.8 fusion.72
  252.8 41.6 %stack.7 = bf16[81,128,2,128]{3,0,2,1:T(8,128)(2,1)} concatenate(bf16[1,128,2,128]{3,0,2,1:T(2,128)(2,1)S(1)} %copy.271, bf16[1,128,2,128]{3,0,2,1:T(2,128)(2,1)S(1)} %copy.272, bf16[1,128,2,128]{3,0,2,1:T(2,128)(2,1)} %copy.273, bf16[1,128,2,128]{3,0,2,1:T(2,128)(2,1)} %copy.274, bf16[1,128,2,128]{3,0,2,1:T(2,128)(2,1)} %copy.275, bf16[1,128,2,128]{3,0,2,1:T(2,128)(2,1)} %copy.276, ...), dimensions={0} | concatenate | bytes 10616832 | tf_op jit(solution)/shard_map/while/body/eval_jaxpr/stack | solution.py:58
  303.1 39.0 %collective-permute-done.4 = bf16[1,16,128,2,128]{4,1,3,2,0:T(8,128)(2,1)S(1)} collective-permute-done((bf16[1,16,128,2,128]{4,1,3,2,0:T(8,128)(2,1)S(1)}, bf16[1,16,128,2,128]{4,1,3,2,0:T(8,128)(2,1)S(1)}, u32[]{:S(2)}, u32[]{:S(2)}) %collective-permute-start.4) | collective-permute-done | bytes 1048608 | tf_op jit(solution)/shard_map/ppermute | solution.py:15
  346.4 7.2 %collective-permute-start.6 = (bf16[4,16,128,1,128]{4,1,3,2,0:T(8,128)(2,1)}, bf16[4,16,128,1,128]{4,1,3,2,0:T(8,128)(2,1)}, u32[]{:S(2)}, u32[]{:S(2)}) collective-permute-start(bf16[4,16,128,1,128]{4,1,3,2,0:T(8,128)(2,1)} %get-tuple-element.230), channel_id=1, source_target_pairs={{0,1},{1,2},{2,3},{3,4},{4,5},{5,6},{6,7},{7,8},{8,9},{9,10},{10,1... | collective-permute-start | bytes 6291464 | tf_op jit(solution)/shard_map/ppermute | solution.py:15
  356.2 41.2 %collective-permute-done.6 = bf16[4,16,128,1,128]{4,1,3,2,0:T(8,128)(2,1)} collective-permute-done((bf16[4,16,128,1,128]{4,1,3,2,0:T(8,128)(2,1)}, bf16[4,16,128,1,128]{4,1,3,2,0:T(8,128)(2,1)}, u32[]{:S(2)}, u32[]{:S(2)}) %collective-permute-start.6) | collective-permute-done | bytes 2097184 | tf_op jit(solution)/shard_map/ppermute | solution.py:15
  397.4 53.6 %collective-permute-done.7 = bf16[4,16,128,1,128]{4,1,3,2,0:T(8,128)(2,1)} collective-permute-done((bf16[4,16,128,1,128]{4,1,3,2,0:T(8,128)(2,1)}, bf16[4,16,128,1,128]{4,1,3,2,0:T(8,128)(2,1)}, u32[]{:S(2)}, u32[]{:S(2)}) %collective-permute-start.7) | collective-permute-done | bytes 2097184 | tf_op jit(solution)/shard_map/ppermute | solution.py:17
  450.9 22.6 %select_maximum_fusion = bf16[4,16,130,4,130]{4,1,3,2,0:T(8,128)(2,1)} fusion(bf16[4,16,128,1,128]{4,1,3,2,0:T(8,128)(2,1)} %collective-permute-done.7, bf16[4,16,128,1,128]{4,1,3,2,0:T(8,128)(2,1)} %collective-permute-done.6, bf16[1,16,128,2,128]{4,1,3,2,0:T(8,128)(2,1)} %copy-done, bf16[2,16,128,2,128]{4,1,3,2,0:T(8,128)(2,1)S(1)} %get-tuple-element.103, ...), kind=kLoop, calls=%fused_computation.165 | loop fusion | flops 116812800 | bytes 17041408 | tf_op jit(solution)/shard_map/concatenate | solution.py:13
  473.5 170.0 %while.25 = (s32[]{:T(128)}, f32[2,128,2,128]{3,2,1,0:T(2,128)S(1)}, s32[2]{0:T(128)S(1)}, bf16[4,16,130,4,130]{4,1,3,2,0:T(8,128)(2,1)}, bf16[16,81]{1,0:T(8,128)(2,1)S(1)}) while((s32[]{:T(128)}, f32[2,128,2,128]{3,2,1,0:T(2,128)S(1)}, s32[2]{0:T(128)S(1)}, bf16[4,16,130,4,130]{4,1,3,2,0:T(8,128)(2,1)}, ...), condition=%wide.region_5.6_spmd.clone, body=%wide.region_4.5_spmd.sunk.clone | while | flops 177840640 | bytes 45699956 | solution.py:103
  475.4 10.5 %convolution_bitcast_fusion.10 = f32[27,130,4,130]{3,0,2,1:T(8,128)} fusion(bf16[4,16,130,4,130]{4,1,3,2,0:T(8,128)(2,1)} %get-tuple-element.615, s32[]{:T(128)S(6)} %select_n.32, bf16[16,81]{1,0:T(8,128)(2,1)S(1)} %get-tuple-element.616), kind=kOutput, calls=%fused_computation.60.clone.1.clone | convolution fusion | flops 58406400 | bytes 11563236 | tf_op jit(solution)/shard_map/while/body/eval_jaxpr/dot_general | solution.py:83
  487.3 10.5 %convolution_bitcast_fusion.9 = f32[27,130,4,130]{3,0,2,1:T(8,128)} fusion(bf16[4,16,130,4,130]{4,1,3,2,0:T(8,128)(2,1)} %get-tuple-element.615, s32[]{:T(128)S(6)} %select_n.31, bf16[16,81]{1,0:T(8,128)(2,1)S(1)} %get-tuple-element.616), kind=kOutput, calls=%fused_computation.59.clone.1.clone | convolution fusion | flops 58406400 | bytes 11563236 | tf_op jit(solution)/shard_map/while/body/eval_jaxpr/dot_general | solution.py:83
  499.7 10.4 %convolution_bitcast_fusion.11 = f32[27,130,4,130]{3,0,2,1:T(8,128)} fusion(bf16[4,16,130,4,130]{4,1,3,2,0:T(8,128)(2,1)} %get-tuple-element.615, s32[]{:T(128)S(6)} %select_n.33, bf16[16,81]{1,0:T(8,128)(2,1)S(1)} %get-tuple-element.616), kind=kOutput, calls=%fused_computation.61.clone.1.clone | convolution fusion | flops 58406400 | bytes 11563236 | tf_op jit(solution)/shard_map/while/body/eval_jaxpr/dot_general | solution.py:83
  510.1 48.3 %slice_add_fusion.82 = f32[1,128,2,128]{3,0,2,1:T(1,128)S(1)} fusion(f32[27,130,4,130]{3,0,2,1:T(8,128)} %convolution_bitcast_fusion.9, f32[27,130,4,130]{3,0,2,1:T(8,128)} %convolution_bitcast_fusion.10, f32[27,130,4,130]{3,0,2,1:T(8,128)} %convolution_bitcast_fusion.11), kind=kLoop, calls=%fused_computation.68.clone.1.clone | loop fusion | flops 2621440 | bytes 10747904 | tf_op jit(solution)/shard_map/while/body/eval_jaxpr/add | solution.py:93
  560.4 10.5 %convolution_bitcast_fusion.10 = f32[27,130,4,130]{3,0,2,1:T(8,128)} fusion(bf16[4,16,130,4,130]{4,1,3,2,0:T(8,128)(2,1)} %get-tuple-element.615, s32[]{:T(128)S(6)} %select_n.32, bf16[16,81]{1,0:T(8,128)(2,1)S(1)} %get-tuple-element.616), kind=kOutput, calls=%fused_computation.60.clone.1.clone | convolution fusion | flops 58406400 | bytes 11563236 | tf_op jit(solution)/shard_map/while/body/eval_jaxpr/dot_general | solution.py:83
  572.3 10.5 %convolution_bitcast_fusion.9 = f32[27,130,4,130]{3,0,2,1:T(8,128)} fusion(bf16[4,16,130,4,130]{4,1,3,2,0:T(8,128)(2,1)} %get-tuple-element.615, s32[]{:T(128)S(6)} %select_n.31, bf16[16,81]{1,0:T(8,128)(2,1)S(1)} %get-tuple-element.616), kind=kOutput, calls=%fused_computation.59.clone.1.clone | convolution fusion | flops 58406400 | bytes 11563236 | tf_op jit(solution)/shard_map/while/body/eval_jaxpr/dot_general | solution.py:83
  584.7 10.4 %convolution_bitcast_fusion.11 = f32[27,130,4,130]{3,0,2,1:T(8,128)} fusion(bf16[4,16,130,4,130]{4,1,3,2,0:T(8,128)(2,1)} %get-tuple-element.615, s32[]{:T(128)S(6)} %select_n.33, bf16[16,81]{1,0:T(8,128)(2,1)S(1)} %get-tuple-element.616), kind=kOutput, calls=%fused_computation.61.clone.1.clone | convolution fusion | flops 58406400 | bytes 11563236 | tf_op jit(solution)/shard_map/while/body/eval_jaxpr/dot_general | solution.py:83
  595.1 48.3 %slice_add_fusion.82 = f32[1,128,2,128]{3,0,2,1:T(1,128)S(1)} fusion(f32[27,130,4,130]{3,0,2,1:T(8,128)} %convolution_bitcast_fusion.9, f32[27,130,4,130]{3,0,2,1:T(8,128)} %convolution_bitcast_fusion.10, f32[27,130,4,130]{3,0,2,1:T(8,128)} %convolution_bitcast_fusion.11), kind=kLoop, calls=%fused_computation.68.clone.1.clone | loop fusion | flops 2621440 | bytes 10747904 | tf_op jit(solution)/shard_map/while/body/eval_jaxpr/add | solution.py:93
  (210 shorter events, 155.7 us)
Async XLA Ops:
  0.0 72.9 %copy-start.3 = (bf16[16,81]{1,0:T(8,128)(2,1)S(1)}, bf16[16,81]{1,0:T(8,128)(2,1)}, u32[]{:S(2)}) copy-start(bf16[16,81]{1,0:T(8,128)(2,1)} %param.12) | copy-start | bytes 7780
  0.0 72.9 %copy-start.4 = (f32[16]{0:T(128)S(1)}, f32[16]{0:T(128)}, u32[]{:S(2)}) copy-start(f32[16]{0:T(128)} %param.13) | copy-start | bytes 196
  2.6 41.5 %all-to-all-start = ((bf16[16,2,8,1024]{3,2,1,0:T(8,128)(2,1)}), bf16[16,2,8,1024]{3,2,1,0:T(8,128)(2,1)S(1)}, u32[]{:S(2)}, u32[]{:S(2)}) async-start(bf16[16,2,8,1024]{3,2,1,0:T(8,128)(2,1)} %stack.4), calls=%async_computation | async-start | bytes 1048576 | tf_op jit(solution)/shard_map/all_to_all | solution.py:32
  44.5 5.2 collective-permute-start
  47.8 9.5 %collective-permute-start.1 = (bf16[1,128,2,128]{3,1,2,0:T(8,128)(2,1)S(1)}, bf16[1,128,2,128]{3,1,2,0:T(8,128)(2,1)S(1)}, u32[]{:S(2)}, u32[]{:S(2)}) collective-permute-start(bf16[1,128,2,128]{3,1,2,0:T(8,128)(2,1)S(1)} %get-tuple-element.237), channel_id=1, source_target_pairs={{16,0},{32,16},{48,32},{64,48},{80,64},{96,80},{112,96},{128,112},... | collective-permute-start | bytes 196616 | tf_op jit(solution)/shard_map/ppermute | solution.py:17
  57.3 8.2 %collective-permute-start.2 = (bf16[4,128,1,128]{3,1,2,0:T(8,128)(2,1)S(1)}, bf16[4,128,1,128]{3,1,2,0:T(8,128)(2,1)S(1)}, u32[]{:S(2)}, u32[]{:S(2)}) collective-permute-start(bf16[4,128,1,128]{3,1,2,0:T(8,128)(2,1)S(1)} %get-tuple-element.234), channel_id=1, source_target_pairs={{0,1},{1,2},{2,3},{3,4},{4,5},{5,6},{6,7},{7,8},{8,9},{9,10},{10,1... | collective-permute-start | bytes 393224 | tf_op jit(solution)/shard_map/ppermute | solution.py:15
  63.6 7.6 %collective-permute-start.3 = (bf16[4,128,1,128]{3,1,2,0:T(8,128)(2,1)S(1)}, bf16[4,128,1,128]{3,1,2,0:T(8,128)(2,1)}, u32[]{:S(2)}, u32[]{:S(2)}) collective-permute-start(bf16[4,128,1,128]{3,1,2,0:T(8,128)(2,1)S(1)} %get-tuple-element.235), channel_id=1, source_target_pairs={{1,0},{2,1},{3,2},{4,3},{5,4},{6,5},{7,6},{8,7},{9,8},{10,9},{11,1... | collective-permute-start | bytes 393224 | tf_op jit(solution)/shard_map/ppermute | solution.py:17
  65.5 0.7 copy-start.2
  298.6 43.5 %collective-permute-start.4 = (bf16[1,16,128,2,128]{4,1,3,2,0:T(8,128)(2,1)S(1)}, bf16[1,16,128,2,128]{4,1,3,2,0:T(8,128)(2,1)S(1)}, u32[]{:S(2)}, u32[]{:S(2)}) collective-permute-start(bf16[1,16,128,2,128]{4,1,3,2,0:T(8,128)(2,1)S(1)} %get-tuple-element.232), channel_id=1, source_target_pairs={{0,16},{16,32},{32,48},{48,64},{64,80},{80,96},{96,112},{112,128},... | collective-permute-start | bytes 3145736 | tf_op jit(solution)/shard_map/ppermute | solution.py:15
  301.2 41.0 %collective-permute-start.5 = (bf16[1,16,128,2,128]{4,1,3,2,0:T(8,128)(2,1)S(1)}, bf16[1,16,128,2,128]{4,1,3,2,0:T(8,128)(2,1)S(1)}, u32[]{:S(2)}, u32[]{:S(2)}) collective-permute-start(bf16[1,16,128,2,128]{4,1,3,2,0:T(8,128)(2,1)S(1)} %get-tuple-element.233), channel_id=1, source_target_pairs={{16,0},{32,16},{48,32},{64,48},{80,64},{96,80},{112,96},{128,112},... | collective-permute-start | bytes 3145736 | tf_op jit(solution)/shard_map/ppermute | solution.py:17
  342.2 1.0 copy-start
  346.4 50.9 %collective-permute-start.6 = (bf16[4,16,128,1,128]{4,1,3,2,0:T(8,128)(2,1)}, bf16[4,16,128,1,128]{4,1,3,2,0:T(8,128)(2,1)}, u32[]{:S(2)}, u32[]{:S(2)}) collective-permute-start(bf16[4,16,128,1,128]{4,1,3,2,0:T(8,128)(2,1)} %get-tuple-element.230), channel_id=1, source_target_pairs={{0,1},{1,2},{2,3},{3,4},{4,5},{5,6},{6,7},{7,8},{8,9},{9,10},{10,1... | collective-permute-start | bytes 6291464 | tf_op jit(solution)/shard_map/ppermute | solution.py:15
  353.6 97.3 %collective-permute-start.7 = (bf16[4,16,128,1,128]{4,1,3,2,0:T(8,128)(2,1)}, bf16[4,16,128,1,128]{4,1,3,2,0:T(8,128)(2,1)}, u32[]{:S(2)}, u32[]{:S(2)}) collective-permute-start(bf16[4,16,128,1,128]{4,1,3,2,0:T(8,128)(2,1)} %get-tuple-element.231), channel_id=1, source_target_pairs={{1,0},{2,1},{3,2},{4,3},{5,4},{6,5},{7,6},{8,7},{9,8},{10,9},{11,1... | collective-permute-start | bytes 6291464 | tf_op jit(solution)/shard_map/ppermute | solution.py:17
  356.2 117.3 %copy-start.1 = (bf16[16,81]{1,0:T(8,128)(2,1)S(1)}, bf16[16,81]{1,0:T(8,128)(2,1)}, u32[]{:S(2)}) copy-start(bf16[16,81]{1,0:T(8,128)(2,1)} %param.14) | copy-start | bytes 7780
